TPU v7x, 32 devices: a whole 2x2x4 slice. The times are simulated.
32 devices in a mesh: blk: 4 (over y, core), batch: 2 (over x), tensor: 4 (over z).
Axes of the slice: x: 2, y: 2, z: 4, core: 2. Of those that a mesh axis runs over, the one named last changes fastest.
Arguments:
- tokens: bfloat16 [6, 512, 768], P('batch', 'blk'), may hold values from -6 to 6
- out_grad: bfloat16 [6, 512, 768], P('batch', 'blk'), may hold values from -6 to 6
- bucket: int32 [6], P('batch'), may hold values from 0 to 1, as said below
- lengths: int32 [6, 4], P('batch'), may hold values from 1 to 512, as said below
- qkv_weight: bfloat16 [1, 3, 768, 768], P(None, None, ('blk', 'batch'), 'tensor'), may hold values from -0.21875 to 0.21875
- qv_bias: float32 [1, 2, 768], P(None, None, 'tensor'), may hold values from -3 to 3
- out_weight: bfloat16 [1, 768, 768], P(None, 'tensor', ('blk', 'batch')), may hold values from -0.625 to 0.625
- ff_in_weight: bfloat16 [1, 768, 3072], P(None, ('blk', 'batch'), 'tensor'), may hold values from -0.21875 to 0.21875
- ff_in_bias: float32 [1, 3072], P(None, 'tensor'), may hold values from -3 to 3
- ff_out_weight: bfloat16 [1, 3072, 768], P(None, 'tensor', ('blk', 'batch')), may hold values from -0.109375 to 0.109375
- branch_bias: float32 [1, 2, 768], replicated, may hold values from -3 to 3
- norm_gain: float32 [1, 2, 768], replicated, may hold values from 0.5 to 1.5
- norm_bias: float32 [1, 2, 768], replicated, may hold values from -3 to 3
Outputs:
- output: bfloat16 [6, 512, 768], P('batch', 'blk')
- tokens_grad: float32 [6, 512, 768], P('batch', 'blk')
- qkv_weight_grad: float32 [1, 3, 768, 768], P(None, None, ('blk', 'batch'), 'tensor')
- qv_bias_grad: float32 [1, 2, 768], P(None, None, 'tensor')
- out_weight_grad: float32 [1, 768, 768], P(None, 'tensor', ('blk', 'batch'))
- ff_in_weight_grad: float32 [1, 768, 3072], P(None, ('blk', 'batch'), 'tensor')
- ff_in_bias_grad: float32 [1, 3072], P(None, 'tensor')
- ff_out_weight_grad: float32 [1, 3072, 768], P(None, 'tensor', ('blk', 'batch'))
- branch_bias_grad: float32 [1, 2, 768], replicated
- norm_gain_grad: float32 [1, 2, 768], replicated
- norm_bias_grad: float32 [1, 2, 768], replicated
- stream_rms: float32 [1, 3], replicated
Inputs may be any that keep to these rules, and one draw needn't show every extreme that they name: Each index of batch holds, among its 3 slots, exactly one of bucket 0, and its length is 512; all other slots are of bucket 1. `lengths`: for a slot of bucket 0 only column 0 counts; for bucket 1 column c is the valid length of the short sequence at positions c * 128 onward, at most 128.
All inputs are finite; a program needn't handle non-finite values.
Results may differ from a plain program's by a relative error of at most 0.019.
Values may be sent and summed in bfloat16 or wider, within the bound.
A program may use at most 64 MiB of HBM per device.

v0:
```python
import jax
import jax.numpy as jnp
from jax import lax
from jax.experimental import pallas as pl
from jax.experimental.pallas import tpu as pltpu
from jax.sharding import PartitionSpec as P

HEAD = 64
SUB = 128


NEG = -1e30


def row_valid(bucket, lengths, pos):
    short = bucket[:, None] != 0
    pick = ((pos // SUB)[:, None] == jnp.arange(lengths.shape[1], dtype=jnp.int32)[None, :]).astype(
        jnp.int32
    )
    short_len = jnp.sum(lengths[:, None, :] * pick[None, :, :], axis=2)
    limit = jnp.where(short, short_len, lengths[:, :1])
    place = jnp.where(short, (pos % SUB)[None, :], pos[None, :])
    return place < limit


def seq_mask(bucket, lengths, qpos, kpos):
    short = bucket[:, None, None] != 0
    same = qpos[:, None] // SUB == kpos[None, :] // SUB
    allowed = jnp.logical_or(jnp.logical_not(short), same[None, :, :])
    return jnp.logical_and(row_valid(bucket, lengths, kpos)[:, None, :], allowed)


def layer_norm(h, gain, shift):
    mean = jnp.mean(h, -1, keepdims=True)
    cent = h - mean
    var = jnp.mean(cent * cent, -1, keepdims=True)
    return cent * lax.rsqrt(var + 1e-12) * gain + shift


def exact_gelu(value):
    return jax.nn.gelu(value, approximate=False)


def general_shards(
    tokens,
    out_grad,
    bucket,
    lengths,
    qkv_weight,
    qv_bias,
    out_weight,
    ff_in_weight,
    ff_in_bias,
    ff_out_weight,
    branch_bias,
    norm_gain,
    norm_bias,
):
    n_seq, rows_blk, width = tokens.shape
    blocks = lax.axis_size("blk")
    rank = lax.axis_index("blk")
    layers = qkv_weight.shape[0]
    local_width = qkv_weight.shape[3]
    heads_here = local_width // HEAD
    total_rows = n_seq * rows_blk
    scale = HEAD ** (-0.5)
    head_shape = (n_seq, rows_blk, heads_here, HEAD)
    qkv_full, out_full, ffin_full, ffout_full = (
        lax.all_gather(qkv_weight, ("blk", "batch"), axis=2, tiled=True),
        lax.all_gather(out_weight, ("blk", "batch"), axis=2, tiled=True),
        lax.all_gather(ff_in_weight, ("blk", "batch"), axis=1, tiled=True),
        lax.all_gather(ff_out_weight, ("blk", "batch"), axis=2, tiled=True),
    )
    local_pos = rank * rows_blk + jnp.arange(rows_blk, dtype=jnp.int32)
    row_ok = row_valid(bucket, lengths, local_pos).astype(jnp.float32).reshape(total_rows, 1)
    whole_pos = jnp.arange(blocks * rows_blk, dtype=jnp.int32)
    sub_bucket, sub_lengths = (bucket, lengths)

    def scores(query, keys, mask):
        found = (
            jnp.einsum("nqhe,nkhe->nhqk", query, keys, preferred_element_type=jnp.float32) * scale
        )
        return jnp.where(mask[:, None], found, NEG)

    x = tokens.astype(jnp.float32).reshape(total_rows, width)
    layer = 0
    xb = x.astype(jnp.bfloat16)
    triple = jnp.einsum("rd,cdk->crk", xb, qkv_full[layer], preferred_element_type=jnp.float32)
    query = (triple[0] + qv_bias[layer, 0]).astype(jnp.bfloat16).reshape(head_shape)
    keys = triple[1].astype(jnp.bfloat16).reshape(head_shape)
    values = (triple[2] + qv_bias[layer, 1]).astype(jnp.bfloat16).reshape(head_shape)
    pair = jnp.stack([keys, values])
    sub_query = query
    sub_pair = pair
    kept = lax.all_gather(sub_pair, "blk", axis=2, tiled=True)
    found = scores(sub_query, kept[0], seq_mask(sub_bucket, sub_lengths, local_pos, whole_pos))
    top = jnp.max(found, -1)
    sub_lse = top + jnp.log(jnp.sum(jnp.exp(found - top[..., None]), -1))
    weights = jnp.exp(found - sub_lse[..., None]).astype(jnp.bfloat16)
    sub_acc = jnp.einsum("nhqk,nkhe->nqhe", weights, kept[1], preferred_element_type=jnp.float32)
    lse = sub_lse
    acc = sub_acc
    att = acc.astype(jnp.bfloat16).reshape(total_rows, local_width)
    a_part = jnp.dot(att, out_full[layer], preferred_element_type=jnp.float32)
    branch = (
        lax.psum(a_part.astype(jnp.bfloat16), "tensor").astype(jnp.float32) + branch_bias[layer, 0]
    )
    upper_in = x + branch
    upper = layer_norm(upper_in, norm_gain[layer, 0], norm_bias[layer, 0])
    upper_b = upper.astype(jnp.bfloat16)
    pre = jnp.dot(upper_b, ffin_full[layer], preferred_element_type=jnp.float32) + ff_in_bias[layer]
    act = exact_gelu(pre).astype(jnp.bfloat16)
    f_part = jnp.dot(act, ffout_full[layer], preferred_element_type=jnp.float32)
    feed = (
        lax.psum(f_part.astype(jnp.bfloat16), "tensor").astype(jnp.float32) + branch_bias[layer, 1]
    )
    lower_in = upper + feed
    squares = [
        jnp.stack(
            [
                jnp.sum(row_ok * x * x),
                jnp.sum(row_ok * branch * branch),
                jnp.sum(row_ok * feed * feed),
            ]
        )
    ]
    saved = [(xb, query, pair, kept, lse, sub_lse, att, acc, upper_in, upper_b, pre, act, lower_in)]
    x = layer_norm(lower_in, norm_gain[layer, 1], norm_bias[layer, 1])
    output = x.astype(jnp.bfloat16).reshape(n_seq, rows_blk, width)
    grad = out_grad.astype(jnp.float32).reshape(total_rows, width)
    g_qkv, g_out, g_in, g_outf = ([], [], [], [])
    g_qvb, g_inb, g_branch, g_gain, g_shift = ([], [], [], [], [])
    for layer in reversed(range(layers)):
        xb, query, pair, kept, lse, sub_lse, att, acc, upper_in, upper_b, pre, act, lower_in = (
            saved[layer]
        )
        _, lower_back = jax.vjp(layer_norm, lower_in, norm_gain[layer, 1], norm_bias[layer, 1])
        d_lower, d_gain2, d_shift2 = lower_back(grad)
        d_feed = d_lower.astype(jnp.bfloat16)
        d_fbias = jnp.sum(d_feed.astype(jnp.float32), 0)
        g_outf.append(jnp.einsum("rf,rd->fd", act, d_feed, preferred_element_type=jnp.float32))
        d_act = jnp.einsum(
            "rd,fd->rf", d_feed, ffout_full[layer], preferred_element_type=jnp.float32
        )
        _, gelu_back = jax.vjp(exact_gelu, pre)
        d_pre = gelu_back(d_act)[0].astype(jnp.bfloat16)
        g_inb.append(jnp.sum(d_pre.astype(jnp.float32), 0))
        g_in.append(jnp.einsum("rd,rf->df", upper_b, d_pre, preferred_element_type=jnp.float32))
        ffn_part = jnp.einsum(
            "rf,df->rd", d_pre, ffin_full[layer], preferred_element_type=jnp.float32
        )
        d_upper = d_lower + lax.psum(ffn_part.astype(jnp.bfloat16), "tensor").astype(jnp.float32)
        _, upper_back = jax.vjp(layer_norm, upper_in, norm_gain[layer, 0], norm_bias[layer, 0])
        d_upper_in, d_gain1, d_shift1 = upper_back(d_upper)
        d_branch = d_upper_in.astype(jnp.bfloat16)
        d_abias = jnp.sum(d_branch.astype(jnp.float32), 0)
        g_out.append(jnp.einsum("rk,rd->kd", att, d_branch, preferred_element_type=jnp.float32))
        d_att = (
            jnp.einsum("rd,kd->rk", d_branch, out_full[layer], preferred_element_type=jnp.float32)
            .astype(jnp.bfloat16)
            .reshape(head_shape)
        )
        delta = jnp.einsum("nqhe,nqhe->nhq", d_att.astype(jnp.float32), acc)
        sub_query, sub_datt, sub_delta = (query, d_att, delta)
        block_keys = kept[0]
        block_found = scores(
            sub_query, block_keys, seq_mask(sub_bucket, sub_lengths, local_pos, whole_pos)
        )
        prob = jnp.exp(block_found - sub_lse[..., None])
        d_prob = jnp.einsum(
            "nqhe,nkhe->nhqk", sub_datt, kept[1], preferred_element_type=jnp.float32
        )
        d_scores = (prob * (d_prob - sub_delta[..., None])).astype(jnp.bfloat16)
        d_query = jnp.einsum(
            "nhqk,nkhe->nqhe", d_scores, block_keys, preferred_element_type=jnp.float32
        )
        d_keys = jnp.einsum(
            "nhqk,nqhe->nkhe", d_scores, sub_query, preferred_element_type=jnp.float32
        )
        d_values = jnp.einsum(
            "nhqk,nqhe->nkhe",
            prob.astype(jnp.bfloat16),
            sub_datt,
            preferred_element_type=jnp.float32,
        )
        sub_dq = d_query
        dpair_all = jnp.stack([d_keys * scale, d_values])
        sub_dpair = lax.psum_scatter(
            dpair_all.astype(jnp.bfloat16), "blk", scatter_dimension=2, tiled=True
        ).astype(jnp.float32)
        d_query, d_pair = (sub_dq, sub_dpair)
        dq_b = (d_query * scale).astype(jnp.bfloat16).reshape(total_rows, local_width)
        dk_b = d_pair[0].astype(jnp.bfloat16).reshape(total_rows, local_width)
        dv_b = d_pair[1].astype(jnp.bfloat16).reshape(total_rows, local_width)
        d_triple = jnp.stack([dq_b, dk_b, dv_b])
        g_qvb.append(
            jnp.stack([jnp.sum(dq_b.astype(jnp.float32), 0), jnp.sum(dv_b.astype(jnp.float32), 0)])
        )
        g_qkv.append(jnp.einsum("rd,crk->cdk", xb, d_triple, preferred_element_type=jnp.float32))
        attn_part = jnp.einsum(
            "crk,cdk->rd", d_triple, qkv_full[layer], preferred_element_type=jnp.float32
        )
        grad = d_upper_in + lax.psum(attn_part.astype(jnp.bfloat16), "tensor").astype(jnp.float32)
        g_branch.append(jnp.stack([d_abias, d_fbias]))
        g_gain.append(jnp.stack([d_gain1, d_gain2]))
        g_shift.append(jnp.stack([d_shift1, d_shift2]))

    def in_order(items):
        return jnp.stack(items[::-1])

    qkv_g, out_g, in_g, outf_g = (
        lax.psum_scatter(in_order(g_qkv), ("blk", "batch"), scatter_dimension=2, tiled=True),
        lax.psum_scatter(in_order(g_out), ("blk", "batch"), scatter_dimension=2, tiled=True),
        lax.psum_scatter(in_order(g_in), ("blk", "batch"), scatter_dimension=1, tiled=True),
        lax.psum_scatter(in_order(g_outf), ("blk", "batch"), scatter_dimension=2, tiled=True),
    )
    count = jnp.sum(row_ok)
    qvb_g, inb_g, branch_g, gain_g, shift_g, square_sums, count_all = lax.psum(
        (
            in_order(g_qvb),
            in_order(g_inb),
            in_order(g_branch),
            in_order(g_gain),
            in_order(g_shift),
            jnp.stack(squares),
            count,
        ),
        ("blk", "batch"),
    )
    rms = jnp.sqrt(square_sums / (count_all * width))
    tokens_grad = grad.reshape(n_seq, rows_blk, width)
    return (
        output,
        tokens_grad,
        qkv_g,
        qvb_g,
        out_g,
        in_g,
        inb_g,
        outf_g,
        branch_g,
        gain_g,
        shift_g,
        rms,
    )


MESH = pl.DeviceIdType.MESH
F32 = jnp.float32
BF16 = jnp.bfloat16
N_SEND = 48
N_RECV = 128


def dot_nn(a, b):
    return lax.dot_general(a, b, (((1,), (0,)), ((), ())), preferred_element_type=F32)


def dot_nt(a, b):
    return lax.dot_general(a, b, (((1,), (1,)), ((), ())), preferred_element_type=F32)


def dot_tn(a, b):
    return lax.dot_general(a, b, (((0,), (0,)), ((), ())), preferred_element_type=F32)


def slot_order(bucket_ref):
    first = jnp.where(bucket_ref[0] == 0, 0, jnp.where(bucket_ref[1] == 0, 1, 2))
    second = jnp.where(first == 0, 1, 0)
    third = jnp.where(first == 2, 1, 2)
    return first, second, third


class Net:
    def __init__(self, send_sems, recv_sems):
        self.send_sems, self.recv_sems = send_sems, recv_sems
        self.copies, self.n_recv = [], 0

    def slot(self):
        self.n_recv += 1
        assert self.n_recv <= N_RECV
        return self.n_recv - 1

    def send(self, src, dst, peer, slot=None):
        at = len(self.copies)
        if at >= N_SEND:
            self.copies[at - N_SEND].wait_send()
        copy = pltpu.make_async_remote_copy(
            src_ref=src,
            dst_ref=dst,
            send_sem=self.send_sems.at[at % N_SEND],
            recv_sem=self.recv_sems.at[self.slot() if slot is None else slot],
            device_id=peer,
            device_id_type=MESH,
        )
        copy.start()
        self.copies.append(copy)
        return copy

    def whole(self, ref, peer, slot):
        return pltpu.make_async_remote_copy(
            src_ref=ref,
            dst_ref=ref,
            send_sem=self.send_sems.at[0],
            recv_sem=self.recv_sems.at[slot],
            device_id=peer,
            device_id_type=MESH,
        )

    def finish(self):
        for copy in self.copies[-N_SEND:]:
            copy.wait_send()


class Gather:
    def __init__(self, net, view, at, near, split=False):
        self.net, self.view, self.near = net, view, near
        self.own, self.x, self.y, self.d, self.size = at
        self.half = self.size // 2
        self.slot = net.slot()
        self.late = net.slot() if split else self.slot

    def part(self, start, size):
        return self.view(pl.ds(pl.multiple_of(start, 16), size))

    def to_core(self, ref, late=False):
        self.net.send(ref, ref, self.near[2], self.late if late else self.slot)

    def issue(self, src=None):
        xnb, ynb, core = self.near
        to = self.part(self.own, self.size)
        src = to if src is None else src
        self.from_x = self.net.send(src, to, xnb)
        self.from_y = self.net.send(src, to, ynb)
        self.net.send(src, to, core, self.slot)

    def forward_x(self):
        xnb, ynb, core = self.near
        self.from_x.wait_recv()
        ref = self.part(self.x, self.half)
        self.first = self.net.send(ref, ref, ynb)
        self.to_core(self.part(self.x, self.size))

    def forward_y(self):
        xnb, ynb, core = self.near
        self.from_y.wait_recv()
        ref = self.part(self.y + self.half, self.half)
        self.second = self.net.send(ref, ref, xnb)
        self.to_core(self.part(self.y, self.size), True)

    def last(self):
        self.first.wait_recv()
        self.second.wait_recv()
        self.to_core(self.part(self.d, self.size), True)

    def ready(self):
        self.net.whole(self.part(0, 4 * self.size), self.near[2], self.slot).wait_recv()

    def ready_half(self, late):
        slot = self.late if late else self.slot
        self.net.whole(self.part(0, 2 * self.size), self.near[2], slot).wait_recv()


class Scatter:
    def __init__(self, net, refs, spot, near):
        self.net, self.spot, self.near = net, spot, near
        self.g, self.d, self.h, self.p1, self.s, self.p2 = refs
        self.rows = self.g.shape[3]
        self.half = self.rows // 2

    def core(self):
        c = self.spot[1]
        self.c1 = self.net.send(self.g.at[:, 1 - c], self.d, self.near[2])

    def first(self):
        yy, c, t = self.spot
        xnb, ynb, _ = self.near
        lo, hi = pl.ds(0, self.half), pl.ds(self.half, self.half)
        self.c1.wait_recv()
        for a in range(2):
            for b in range(2):
                self.h[a, b] = (self.g[a, c, b].astype(F32) + self.d[a, b].astype(F32)).astype(BF16)
        self.px = self.net.send(self.h.at[:, 1 - t, lo], self.p1.at[0], xnb)
        self.py = self.net.send(self.h.at[1 - yy, :, hi], self.p1.at[1], ynb)

    def second_x(self):
        yy, c, t = self.spot
        xnb, ynb, _ = self.near
        lo = pl.ds(0, self.half)
        self.px.wait_recv()
        self.s[0] = (self.h[1 - yy, t, lo].astype(F32) + self.p1[0, 1 - yy].astype(F32)).astype(BF16)
        self.qy = self.net.send(self.s.at[0], self.p2.at[0], ynb)

    def second_y(self):
        yy, c, t = self.spot
        xnb, ynb, _ = self.near
        hi = pl.ds(self.half, self.half)
        self.py.wait_recv()
        self.s[1] = (self.h[yy, 1 - t, hi].astype(F32) + self.p1[1, 1 - t].astype(F32)).astype(BF16)
        self.qx = self.net.send(self.s.at[1], self.p2.at[1], xnb)

    def result(self):
        yy, c, t = self.spot
        self.qy.wait_recv()
        self.qx.wait_recv()
        lo, hi = pl.ds(0, self.half), pl.ds(self.half, self.half)
        low = self.h[yy, t, lo].astype(F32) + self.p1[0, yy].astype(F32) + self.p2[0].astype(F32)
        high = self.h[yy, t, hi].astype(F32) + self.p1[1, t].astype(F32) + self.p2[1].astype(F32)
        return low, high


def fused_kernel(*refs):
    (
        bucket, lengths, tokens, out_grad, qkv_w, out_w, ffi_w, ffo_w, qv_bias, ffi_b, br_bias, gain, shift,
        out_hbm, tg_hbm, gq_hbm, go_hbm, gi_hbm, gf_hbm, vec_hbm, qvb_hbm,
        tok, cot, w_q, w_o, w_i, w_f, own_o, bias_r, own_q, xs, xs_t, q_r, kv_r, kv_a, p_a, p_b,
        att, att_r, ps, pr, xh1, rstd1, yb, act, gp, dh2, dfb, dab, df_t, yb_t, dpre, dh1, da_t,
        datt, datt_s, dkv_s, dkv_c, dkv_t, dkv_y, dtri, dx_p, dx_s, dx_1, dx_2, dx_t,
        sc_q, sc_o, sc_i, sc_f, z_o, z_i, z_f, t_o, t_i, t_f, vs, vr, vz, qs, qr,
        out_v, tg_v, gq_v, go_v, gi_v, gf_v, vec_v, qvb_v,
        local_sems, send_sems, recv_sems,
    ) = refs
    n_seq, n_rows, width = tok.shape
    blk_rows = ffi_w.shape[0]
    head_w = qkv_w.shape[2]
    pair_w = 2 * head_w
    heads = head_w // HEAD
    half, quart = n_rows // 2, n_rows // 4
    tile = 256
    n_tile = width // tile
    scale = HEAD ** (-0.5)

    r = lax.axis_index("blk")
    t = lax.axis_index("batch")
    z = lax.axis_index("tensor")
    yy, c = r // 2, r % 2
    pz, qz = z // 2, z % 2
    r1, r2 = r + 1 - 2 * c, (r + 2) % 4
    z1, z2 = z + 1 - 2 * qz, (z + 2) % 4
    core, xnb, ynb = (r1, t, z), (r, 1 - t, z), (r2, t, z)
    zn1, zn2 = (r, t, z1), (r, t, z2)
    peers = (zn2, zn1, xnb, ynb, core)
    near = (xnb, ynb, core)

    barrier = pltpu.get_barrier_semaphore()
    for peer in peers:
        pl.semaphore_signal(barrier, inc=1, device_id=peer, device_id_type=MESH)

    net = Net(send_sems, recv_sems)

    def block(rr, tt):
        return (rr * 2 + tt) * blk_rows

    at = (block(r, t), block(r, 1 - t), block(r2, t), block(r2, 1 - t), blk_rows)
    own = pl.ds(pl.multiple_of(block(r, t), 32), blk_rows)

    def gather(view, split=False):
        return Gather(net, view, at, near, split)

    ga_q = gather(lambda rows: w_q.at[rows])
    ga_o = [gather(lambda rows, k=k: w_o.at[k, rows]) for k in range(2)]
    ga_i = [gather(lambda rows, k=k: w_i.at[k, rows]) for k in range(2)]
    ga_f = [gather(lambda rows, k=k: w_f.at[k, rows], True) for k in range(2)]

    local = [
        pltpu.make_async_copy(src, dst, local_sems.at[k])
        for k, (src, dst) in enumerate(
            (
                (out_w, own_o),
                (tokens, tok),
                (qkv_w, own_q),
                (ffi_w, w_i.at[0, own]),
                (ffo_w, w_f.at[0, own]),
                (out_grad, cot),
            )
        )
    ]
    for copy in local:
        copy.start()
    stores = []

    def store(src, dst):
        copy = pltpu.make_async_copy(src, dst, local_sems.at[len(local) + len(stores)])
        copy.start()
        stores.append(copy)

    st = {}

    order = slot_order(bucket)

    def weights_first():
        local[0].wait()
        w_o[0, own] = jnp.transpose(own_o[...])
        local[2].wait()
        w_q[own] = jnp.concatenate([own_q[1], own_q[2], own_q[0]], 1)
        local[1].wait()
        for s in range(n_seq):
            xs[s * n_rows : (s + 1) * n_rows] = tok[order[s]]

    def enter():
        pl.semaphore_wait(barrier, len(peers))

    def far_weight(kind, src, buf):
        st["z" + kind] = net.send(src, buf.at[1, own], zn2)
        if kind == "i":
            st["zb"] = net.send(ffi_b, bias_r, zn2)

    def issue_second(kind, gather):
        st["z" + kind].wait_recv()
        gather.issue()

    def turn_x():
        xs_t[...] = jnp.transpose(xs[...])

    def keys_of(rr):
        return kv_a.at[pl.ds(pl.multiple_of(rr * n_rows, n_rows), n_rows)]

    def keys_values():
        ga_q.ready()
        bias = jnp.concatenate([jnp.zeros((1, head_w), F32), qv_bias[1:2, :]], 1)
        kv_r[...] = (dot_nn(xs[...], w_q[:, 0:pair_w]) + bias).astype(BF16)
        kv_a[pl.ds(pl.multiple_of(r * n_rows, n_rows), n_rows)] = kv_r[0:n_rows]
        st["kv_y"] = net.send(keys_of(r), keys_of(r), ynb)
        st["kv_c"] = [net.send(keys_of(r), keys_of(r), core)]

    def keys_pass():
        st["kv_y"].wait_recv()
        st["kv_c"].append(net.send(keys_of(r2), keys_of(r2), core))

    def queries():
        q_r[...] = (dot_nn(xs[...], w_q[:, pair_w:]) + qv_bias[0:1, :]).astype(BF16)

    lane_head = lax.broadcasted_iota(jnp.int32, (1, head_w), 1) // HEAD

    def of_head(value, h):
        return jnp.where(lane_head == h, value, jnp.zeros_like(value))

    def limit_of(s):
        index = order[s]
        return lengths[index, r], lengths[index, 0]

    own_half = pl.ds(pl.multiple_of(pz * half, half), half)
    other_half = pl.ds(pl.multiple_of((1 - pz) * half, half), half)
    key_at = lax.broadcasted_iota(jnp.int32, (1, n_rows), 1)

    def rows_at(s):
        return slice(s * n_rows, (s + 1) * n_rows)

    def few_at(s):
        return slice(s * half, (s + 1) * half)

    def attend(s):
        if s == 0:
            for copy in st["kv_c"]:
                copy.wait_recv()
            both, probs, key_ok = kv_a[...], p_a, None
        else:
            both, probs = kv_r[rows_at(s)], p_b.at[s - 1]
            key_ok = key_at < limit_of(s)[0]
        keys, values = both[:, 0:head_w], both[:, head_w:pair_w]
        query = q_r[rows_at(s)]
        total = jnp.zeros((n_rows, head_w), F32)
        for h in range(heads):
            score = dot_nt(of_head(query, h), keys) * scale
            if key_ok is not None:
                score = jnp.where(key_ok, score, NEG)
            e = jnp.exp(score - jnp.max(score, -1, keepdims=True))
            prob = e / jnp.sum(e, -1, keepdims=True)
            probs[h] = prob
            total = total + dot_nn(prob.astype(BF16), of_head(values, h))
        att[s] = total.astype(BF16)
        st["att", s] = net.send(att.at[s, other_half], att_r.at[s], zn2)

    def pair_send(k, s, value):
        ps[k, s] = value.astype(BF16)
        st["pair", k, s] = net.send(ps.at[k, s], pr.at[k, s], zn1)

    def pair_sum(k, s):
        st["pair", k, s].wait_recv()
        return ps[k, s].astype(F32) + pr[k, s].astype(F32)

    def ready(kind, gathers):
        if ("ready", kind) not in st:
            st["ready", kind] = True
            for gather in gathers:
                gather.ready()

    def project(s):
        ready("o", ga_o)
        st["att", s].wait_recv()
        pair_send(0, s, dot_nt(att[s, own_half], w_o[0]) + dot_nt(att_r[s], w_o[1]))

    vec = {k: jnp.zeros((1, width), F32) for k in range(12)}
    row_at = lax.broadcasted_iota(jnp.int32, (half, 1), 0)

    def row_ok(s):
        short, full = limit_of(s)
        place = row_at + pz * half
        ok = place + r * n_rows < full if s == 0 else place < short
        return ok.astype(F32)

    def tally(k, value):
        vec[k] = vec[k] + jnp.sum(value, 0, keepdims=True)

    def mean_of(value):
        return jnp.mean(value, -1, keepdims=True)

    def normed(h):
        cent = h - mean_of(h)
        rstd = lax.rsqrt(mean_of(cent * cent) + 1e-12)
        return cent * rstd, rstd

    def first_norm(s):
        here = few_at(s)
        x = xs[pl.ds(pl.multiple_of(s * n_rows + pz * half, half), half)].astype(F32)
        branch = pair_sum(0, s) + br_bias[0:1, :]
        ok = row_ok(s)
        tally(8, ok * (x * x))
        tally(9, ok * (branch * branch))
        tally(11, ok * jnp.ones((1, width), F32))
        hat, rstd = normed(x + branch)
        xh1[here] = hat
        rstd1[here] = rstd
        yb[here] = (hat * gain[0:1, :] + shift[0:1, :]).astype(BF16)

    def turn_y():
        yb_t[...] = jnp.transpose(yb[...])

    def hidden(s):
        if ("ready", "i") not in st:
            st["zb"].wait_recv()
            local[3].wait()
        ready("i", ga_i)
        here = few_at(s)
        for k in range(2):
            for n in range(n_tile):
                cols = slice(n * tile, (n + 1) * tile)
                bias = ffi_b[:, cols] if k == 0 else bias_r[:, cols]
                pre = dot_nn(yb[here], w_i[k, :, cols]) + bias
                phi = 0.5 * (1.0 + lax.erf(pre * (0.5**0.5)))
                act[k, here, cols] = (pre * phi).astype(BF16)
                gp[k, here, cols] = phi + pre * (jnp.exp(-0.5 * pre * pre) * 0.3989422804014327)

    def feed_out(late, s):
        if ("feed", late) not in st:
            st["feed", late] = True
            if not late:
                local[4].wait()
            for gather in ga_f:
                gather.ready_half(late)
        here = few_at(s)
        side = width // 2
        cols = pl.ds(pl.multiple_of(((1 - yy) if late else yy) * side, 128), side)
        value = dot_nt(act[0, here], w_f[0, cols]) + dot_nt(act[1, here], w_f[1, cols])
        ps[1, s, :, cols] = value.astype(BF16)
        st["feed", late, s] = net.send(ps.at[1, s, :, cols], pr.at[1, s, :, cols], zn1)

    def second_norm(s):
        here = few_at(s)
        if "cot" not in st:
            st["cot"] = True
            local[5].wait()
        for late in range(2):
            st["feed", late, s].wait_recv()
        feed = ps[1, s].astype(F32) + pr[1, s].astype(F32) + br_bias[1:2, :]
        tally(10, row_ok(s) * (feed * feed))
        hat, rstd = normed(xh1[here] * gain[0:1, :] + shift[0:1, :] + feed)
        out_v[s, own_half] = (hat * gain[1:2, :] + shift[1:2, :]).astype(BF16)
        g = cot[order[s], own_half].astype(F32)
        tally(1, g * hat)
        tally(2, g)
        g = g * gain[1:2, :]
        d = rstd * (g - mean_of(g) - hat * mean_of(g * hat))
        dh2[here] = d
        d = d.astype(BF16)
        dfb[here] = d
        tally(0, d.astype(F32))
        total = jnp.zeros((half, width), F32)
        for k in range(2):
            p = (dot_nn(d, w_f[k]) * gp[k, here]).astype(BF16)
            dpre[k, here] = p
            tally(3 + k, p.astype(F32))
            total = total + dot_nt(p, w_i[k])
        pair_send(2, s, total)

    quarter = pl.ds(pl.multiple_of(z * quart, quart), quart)
    quarter_2 = pl.ds(pl.multiple_of(z2 * quart, quart), quart)

    def out_far(s):
        here = out_v.at[s, quarter]
        st["out2", s] = net.send(here, here, zn2)

    def out_near(s):
        st["out2", s].wait_recv()
        there = out_v.at[s, quarter_2]
        st["out1", s] = net.send(there, there, zn1)

    def scatter(refs, k=None):
        views = refs if k is None else [ref.at[k] for ref in refs]
        return Scatter(net, views, (yy, c, t), near)

    rs_f = [scatter(sc_f, k) for k in range(2)]
    rs_i = [scatter(sc_i, k) for k in range(2)]
    rs_o = [scatter(sc_o, k) for k in range(2)]
    rs_q = scatter(sc_q)

    def grads(lhs, rhs, out):
        value = dot_nn(lhs, rhs).astype(BF16)
        for b in range(8):
            piece = value[b * blk_rows : (b + 1) * blk_rows]
            out[b // 4, (b // 2) % 2, b % 2] = piece

    def grads_wide(left, right, rs):
        for n in range(n_tile):
            cols = slice(n * tile, (n + 1) * tile)
            grads(left[...], right[:, cols], rs.g.at[:, :, :, :, cols])
        rs.core()

    def grad_f(k):
        if k == 1:
            df_t[...] = jnp.transpose(dfb[...])
        grads_wide(df_t, act.at[k], rs_f[k])

    def grad_i(k):
        grads_wide(yb_t, dpre.at[k], rs_i[k])

    def grad_o():
        da_t[...] = jnp.transpose(dab[...])
        rows_l = jnp.concatenate([att[s, own_half] for s in range(n_seq)], 0)
        rows_r = jnp.concatenate([att_r[s] for s in range(n_seq)], 0)
        grads(da_t[...], rows_r, rs_o[1].g)
        rs_o[1].core()
        grads(da_t[...], rows_l, rs_o[0].g)
        rs_o[0].core()

    def grad_q():
        grads(xs_t[...], dtri[...], rs_q.g)
        rs_q.core()

    def first_norm_back(s):
        here = few_at(s)
        hat = xh1[here]
        g = dh2[here] + pair_sum(2, s)
        tally(6, g * hat)
        tally(7, g)
        g = g * gain[0:1, :]
        d = rstd1[here] * (g - mean_of(g) - hat * mean_of(g * hat))
        dh1[here] = d
        d = d.astype(BF16)
        dab[here] = d
        tally(5, d.astype(F32))
        datt_s[s] = dot_nn(d, w_o[1]).astype(BF16)
        st["datt", s] = net.send(datt_s.at[s], datt.at[s, own_half], zn2)
        datt[s, own_half] = dot_nn(d, w_o[0]).astype(BF16)

    def vec_step(k):
        if k == 0:
            for n in range(12):
                vs[0, n : n + 1] = vec[n]
            vs[0, 12:16] = jnp.zeros((4, width), F32)
        else:
            st["vec"].wait_recv()
            vs[k] = vs[k - 1] + vr[k - 1]
        if k < 3:
            st["vec"] = net.send(vs.at[k], vr.at[k], (core, xnb, ynb)[k])
            return
        lane = lax.broadcasted_iota(jnp.int32, (1, width), 1)
        last = jnp.zeros((1, width), F32)
        for n in range(4):
            last = jnp.where(lane == n, jnp.sum(vs[3, 8 + n : 9 + n], 1, keepdims=True), last)
        vz[0, 0:3] = vs[3, 0:3]
        vz[0, 3:4] = vs[3, 4:5]
        vz[0, 4:7] = vs[3, 5:8]
        vz[0, 7:8] = last
        st["vec"] = net.send(vz.at[0], vz.at[1], zn2)

    def attend_back(s):
        st["datt", s].wait_recv()
        if s == 0:
            both, probs = kv_a[...], p_a
        else:
            both, probs = kv_r[rows_at(s)], p_b.at[s - 1]
        keys, values = both[:, 0:head_w], both[:, head_w:pair_w]
        query = q_r[rows_at(s)]
        d_att = datt[s]
        dq = jnp.zeros((n_rows, head_w), F32)
        dk = jnp.zeros(keys.shape, F32)
        dv = jnp.zeros(keys.shape, F32)
        for h in range(heads):
            prob = probs[h]
            d_h = of_head(d_att, h)
            dp = dot_nt(d_h, values)
            delta = jnp.sum(prob * dp, -1, keepdims=True)
            ds = (prob * (dp - delta)).astype(BF16)
            dq = dq + dot_nn(ds, of_head(keys, h))
            dk = dk + dot_tn(ds, of_head(query, h))
            dv = dv + dot_tn(prob.astype(BF16), d_h)
        dtri[rows_at(s), pair_w:] = (dq * scale).astype(BF16)
        both = jnp.concatenate([(dk * scale).astype(BF16), dv.astype(BF16)], 1)
        if s == 0:
            for a in range(4):
                dkv_s[a // 2, a % 2] = both[rows_at(a)]
            st["dkv1"] = net.send(dkv_s.at[:, 1 - c], dkv_c, core)
        else:
            dtri[rows_at(s), 0:pair_w] = both

    def keys_back():
        st["dkv1"].wait_recv()
        dkv_t[...] = (dkv_s[1 - yy, c].astype(F32) + dkv_c[1 - yy].astype(F32)).astype(BF16)
        st["dkv2"] = net.send(dkv_t, dkv_y, ynb)

    def dx_of(s):
        total = dot_nt(dtri[rows_at(s)], w_q[...])
        dx_p[s] = total
        for a in range(4):
            dx_s[a // 2, a % 2, s] = total[a * quart : (a + 1) * quart].astype(BF16)

    def half_rows(s):
        return pl.ds(pl.multiple_of(s * half + qz * quart, quart), quart)

    groups = {"b": (1, n_seq), "a": (0, 1)}

    def dx_first(group):
        lo, hi = groups[group]
        if group == "a":
            st["dkv2"].wait_recv()
            total = dkv_s[yy, c].astype(F32) + dkv_c[yy].astype(F32) + dkv_y[...].astype(F32)
            dtri[0:n_rows, 0:pair_w] = total.astype(BF16)
        for s in range(lo, hi):
            dx_of(s)
        st[group, 1] = net.send(dx_s.at[:, 1 - qz, lo:hi], dx_1.at[:, lo:hi], zn1)

    def dx_second(group):
        lo, hi = groups[group]
        st[group, 1].wait_recv()
        for s in range(lo, hi):
            dx_t[s] = (dx_p[s, quarter_2] + dx_1[1 - pz, s].astype(F32)).astype(BF16)
        st[group, 2] = net.send(dx_t.at[lo:hi], dx_2.at[lo:hi], zn2)

    def dx_third(group):
        lo, hi = groups[group]
        st[group, 2].wait_recv()
        for s in range(lo, hi):
            total = dx_p[s, quarter] + dx_1[pz, s].astype(F32) + dx_2[s].astype(F32)
            tg_v[s, quarter] = (total + dh1[half_rows(s)]).astype(BF16)
        here = tg_v.at[lo:hi, quarter]
        st[group, 3], st[group, 4] = net.send(here, here, zn2), net.send(here, here, zn1)

    def dx_last(group):
        lo, hi = groups[group]
        st[group, 3].wait_recv()
        there = tg_v.at[lo:hi, quarter_2]
        st[group, 5] = net.send(there, there, zn1)

    def bias_step(k):
        if k == 0:
            qs[0] = jnp.zeros(qs.shape[1:], F32)
            total = jnp.sum(dtri[...].astype(F32), 0, keepdims=True)
            qs[0, 0:1] = total[:, pair_w:]
            qs[0, 1:2] = total[:, head_w:pair_w]
        else:
            st["bias"].wait_recv()
            qs[k] = qs[k - 1] + qr[k - 1]
        st["bias"] = net.send(qs.at[k], qr.at[k], (core, xnb, ynb)[k])

    def to_z(kind, rs, buf, got):
        low, high = rs.result()
        n = low.shape[0]
        buf[0:n] = low.astype(BF16)
        buf[n : 2 * n] = high.astype(BF16)
        st["g" + kind] = net.send(buf, got, zn2)

    def put(kind, rs, out, to, got=None):
        low, high = rs.result()
        n = low.shape[0]
        if got is not None:
            st["g" + kind].wait_recv()
            low = low + got[0:n].astype(F32)
            high = high + got[n : 2 * n].astype(F32)
        out[0:n] = low
        out[n : 2 * n] = high
        store(out, to)

    def out_store():
        for s in range(n_seq):
            st["out1", s].wait_recv()
        store(out_v, out_hbm)

    def vec_store():
        st["vec"].wait_recv()
        vec_v[...] = vz[0] + vz[1]
        vec_v[3:4] = vs[3, 3:4] + vz[1, 3:4]
        store(vec_v, vec_hbm)

    def bias_store():
        st["bias"].wait_recv()
        qvb_v[...] = qs[2] + qr[2]
        store(qvb_v, qvb_hbm)

    def dx_store():
        for group in groups:
            for k in (4, 5):
                st[group, k].wait_recv()
        store(tg_v, tg_hbm)

    weights_first()
    enter()
    far_weight("o", w_o.at[0, own], w_o)
    ga_q.issue()
    ga_i[0].issue(ffi_w)
    far_weight("i", ffi_w, w_i)
    ga_q.forward_y()
    ga_q.forward_x()
    ga_o[0].issue()
    issue_second("o", ga_o[1])
    ga_f[0].issue(ffo_w)
    ga_i[0].forward_y()
    far_weight("f", ffo_w, w_f)
    ga_q.last()
    keys_values()
    queries()
    ga_o[0].forward_x()
    ga_o[1].forward_y()
    attend(1)
    ga_o[1].forward_x()
    issue_second("i", ga_i[1])
    ga_o[0].forward_y()
    attend(2)
    ga_i[0].forward_x()
    keys_pass()
    attend(0)
    issue_second("f", ga_f[1])
    ga_i[1].forward_x()
    ga_o[0].last()
    ga_f[0].forward_x()
    ga_o[1].last()
    project(2)
    ga_i[1].forward_y()
    project(1)
    ga_i[0].last()
    ga_f[0].forward_y()
    ga_f[1].forward_x()
    project(0)
    ga_f[1].forward_y()
    turn_x()
    ga_i[1].last()
    first_norm(2)
    hidden(2)
    ga_f[0].last()
    feed_out(0, 2)
    first_norm(1)
    hidden(1)
    ga_f[1].last()
    feed_out(0, 1)
    feed_out(1, 1)
    first_norm(0)
    feed_out(1, 2)
    hidden(0)
    feed_out(0, 0)
    feed_out(1, 0)
    second_norm(1)
    second_norm(2)
    second_norm(0)
    out_far(1)
    grad_f(1)
    turn_y()
    grad_i(0)
    rs_f[1].first()
    first_norm_back(1)
    first_norm_back(2)
    grad_i(1)
    first_norm_back(0)
    vec_step(0)
    vec_step(1)
    out_far(0)
    rs_f[1].second_y()
    rs_f[1].second_x()
    out_near(1)
    attend_back(1)
    rs_i[0].first()
    out_far(2)
    attend_back(2)
    dx_first("b")
    attend_back(0)
    grad_o()
    to_z("f", rs_f[1], t_f, z_f)
    keys_back()
    rs_o[1].first()
    rs_i[0].second_y()
    rs_i[1].first()
    dx_first("a")
    rs_o[0].first()
    grad_f(0)
    rs_o[1].second_y()
    dx_second("b")
    out_near(0)
    rs_o[1].second_x()
    bias_step(0)
    rs_f[0].first()
    dx_second("a")
    bias_step(1)
    vec_step(2)
    rs_i[0].second_x()
    rs_i[1].second_y()
    rs_i[1].second_x()
    dx_third("b")
    dx_third("a")
    grad_q()
    rs_q.first()
    to_z("o", rs_o[1], t_o, z_o)
    bias_step(2)
    out_near(2)
    rs_f[0].second_y()
    to_z("i", rs_i[1], t_i, z_i)
    dx_last("b")
    rs_o[0].second_x()
    rs_f[0].second_x()
    rs_o[0].second_y()
    dx_last("a")
    vec_step(3)
    rs_q.second_y()
    out_store()
    bias_store()
    rs_q.second_x()
    put("f", rs_f[0], gf_v, gf_hbm, z_f)
    put("q", rs_q, gq_v, gq_hbm)
    put("o", rs_o[0], go_v, go_hbm, z_o)
    dx_store()
    put("i", rs_i[0], gi_v, gi_hbm, z_i)
    vec_store()

    for copy in stores:
        copy.wait()
    net.finish()


def finish_kernel(
    bucket,
    out_i,
    tg_i,
    gq_i,
    go_i,
    gi_i,
    gf_i,
    vec_i,
    qvb_i,
    out_o,
    tg_o,
    gq_o,
    qvb_o,
    go_o,
    gi_o,
    inb_o,
    gf_o,
    br_o,
    gain_o,
    shift_o,
    rms_o,
):
    order = slot_order(bucket)
    for s in range(3):
        at = jnp.where(order[0] == s, 0, jnp.where(order[1] == s, 1, 2))
        out_o[s] = out_i[at]
        tg_o[s] = tg_i[at].astype(F32)
    n = gq_o.shape[2]
    value = gq_i[...]
    for k, part in enumerate((1, 2, 0)):
        gq_o[part] = value[:, k * n : (k + 1) * n]
    go_o[...] = jnp.transpose(go_i[...])
    gi_o[...] = gi_i[...]
    gf_o[...] = gf_i[...]
    qvb_o[...] = qvb_i[0:2]
    inb_o[...] = vec_i[3:4]
    br_o[0:1] = vec_i[4:5]
    br_o[1:2] = vec_i[0:1]
    gain_o[0:1] = vec_i[5:6]
    gain_o[1:2] = vec_i[1:2]
    shift_o[0:1] = vec_i[6:7]
    shift_o[1:2] = vec_i[2:3]
    rms_o[...] = jnp.sqrt(vec_i[7:8, 0:3] / vec_i[7:8, 3:4])


def fused_shards(
    tokens,
    out_grad,
    bucket,
    lengths,
    qkv_weight,
    qv_bias,
    out_weight,
    ff_in_weight,
    ff_in_bias,
    ff_out_weight,
    branch_bias,
    norm_gain,
    norm_bias,
):
    n_seq, n_rows, width = tokens.shape
    blk_rows, head_w = qkv_weight.shape[2:]
    ff = ff_in_weight.shape[2]
    heads = head_w // HEAD
    rows = n_seq * n_rows
    half, quart = n_rows // 2, n_rows // 4
    few = n_seq * half
    keys = 4 * n_rows
    vmem = pl.BlockSpec(memory_space=pltpu.VMEM)
    smem = pl.BlockSpec(memory_space=pltpu.SMEM)
    hbm = pl.BlockSpec(memory_space=pl.ANY)

    def v(*shape, dtype=BF16):
        return pltpu.VMEM(shape, dtype)

    def f(*shape):
        return pltpu.VMEM(shape, F32)

    wide = {"q": (blk_rows, 3 * head_w), "o": (blk_rows, head_w), "i": (blk_rows, ff), "f": (blk_rows, ff)}

    def scatter_bufs(kind):
        n, cols = wide[kind]
        lead = () if kind == "q" else (2,)
        dims = ((2, 2, 2, n), (2, 2, n), (2, 2, n), (2, 2, n // 2), (2, n // 2), (2, n // 2))
        return [v(*lead, *dim, cols) for dim in dims]

    scratch = [
        v(n_seq, n_rows, width),
        v(n_seq, n_rows, width),
        v(width, 3 * head_w),
        v(2, width, head_w),
        v(2, width, ff),
        v(2, width, ff),
        v(head_w, blk_rows),
        f(1, ff),
        v(3, blk_rows, head_w),
        v(rows, width),
        v(width, rows),
        v(rows, head_w),
        v(rows, 2 * head_w),
        v(keys, 2 * head_w),
        f(heads, n_rows, keys),
        f(n_seq - 1, heads, n_rows, n_rows),
        v(n_seq, n_rows, head_w),
        v(n_seq, half, head_w),
        v(3, n_seq, half, width),
        v(3, n_seq, half, width),
        f(few, width),
        f(few, 1),
        v(few, width),
        v(2, few, ff),
        f(2, few, ff),
        f(few, width),
        v(few, width),
        v(few, width),
        v(width, few),
        v(width, few),
        v(2, few, ff),
        f(few, width),
        v(width, few),
        v(n_seq, n_rows, head_w),
        v(n_seq, half, head_w),
        v(2, 2, n_rows, 2 * head_w),
        v(2, n_rows, 2 * head_w),
        v(n_rows, 2 * head_w),
        v(n_rows, 2 * head_w),
        v(rows, 3 * head_w),
        f(n_seq, n_rows, width),
        v(2, 2, n_seq, quart, width),
        v(2, n_seq, quart, width),
        v(n_seq, quart, width),
        v(n_seq, quart, width),
        scatter_bufs("q"),
        scatter_bufs("o"),
        scatter_bufs("i"),
        scatter_bufs("f"),
        v(*wide["o"]),
        v(*wide["i"]),
        v(*wide["f"]),
        v(*wide["o"]),
        v(*wide["i"]),
        v(*wide["f"]),
        f(4, 16, width),
        f(3, 16, width),
        f(2, 8, width),
        f(3, 8, head_w),
        f(3, 8, head_w),
        v(n_seq, n_rows, width),
        v(n_seq, n_rows, width),
        f(*wide["q"]),
        f(*wide["o"]),
        f(*wide["i"]),
        f(*wide["f"]),
        f(8, width),
        f(8, head_w),
        pltpu.SemaphoreType.DMA((14,)),
        pltpu.SemaphoreType.DMA((N_SEND,)),
        pltpu.SemaphoreType.DMA((N_RECV,)),
    ]

    def shape(*dims, dtype=F32):
        return jax.ShapeDtypeStruct(dims, dtype)

    main_out = [
        shape(n_seq, n_rows, width, dtype=BF16),
        shape(n_seq, n_rows, width, dtype=BF16),
        shape(*wide["q"]),
        shape(*wide["o"]),
        shape(*wide["i"]),
        shape(*wide["f"]),
        shape(8, width),
        shape(8, head_w),
    ]
    results = pl.pallas_call(
        fused_kernel,
        out_shape=main_out,
        in_specs=[smem, smem] + [hbm] * 6 + [vmem] * 5,
        out_specs=[hbm] * 8,
        scratch_shapes=scratch,
        compiler_params=pltpu.CompilerParams(
            collective_id=0, has_side_effects=True, vmem_limit_bytes=60 * 2**20
        ),
        name="encoder_layer",
    )(
        bucket,
        lengths,
        tokens,
        out_grad,
        qkv_weight[0],
        out_weight[0],
        ff_in_weight[0],
        jnp.transpose(ff_out_weight[0]),
        qv_bias[0],
        ff_in_bias,
        branch_bias[0],
        norm_gain[0],
        norm_bias[0],
    )
    final = pl.pallas_call(
        finish_kernel,
        out_shape=[
            shape(n_seq, n_rows, width, dtype=BF16),
            shape(n_seq, n_rows, width),
            shape(3, blk_rows, head_w),
            shape(2, head_w),
            shape(head_w, blk_rows),
            shape(blk_rows, ff),
            shape(1, ff),
            shape(blk_rows, ff),
            shape(2, width),
            shape(2, width),
            shape(2, width),
            shape(1, 3),
        ],
        in_specs=[smem] + [vmem] * 8,
        out_specs=[vmem] * 12,
        compiler_params=pltpu.CompilerParams(vmem_limit_bytes=60 * 2**20),
        name="finish",
    )(bucket, *results)
    out, tg, gq, qvb, go, gi, inb, gf, br, gain, shift, rms = final
    return (
        out,
        tg,
        gq[None],
        qvb[None],
        go[None],
        gi[None],
        inb,
        jnp.transpose(gf)[None],
        br[None],
        gain[None],
        shift[None],
        rms,
    )


def solution(mesh):
    placed = (
        P("batch", "blk", None),
        P("batch", "blk", None),
        P("batch"),
        P("batch", None),
        P(None, None, ("blk", "batch"), "tensor"),
        P(None, None, "tensor"),
        P(None, "tensor", ("blk", "batch")),
        P(None, ("blk", "batch"), "tensor"),
        P(None, "tensor"),
        P(None, "tensor", ("blk", "batch")),
        P(),
        P(),
        P(),
    )
    sizes = (mesh.shape["blk"], mesh.shape["batch"], mesh.shape["tensor"])
    body = fused_shards if sizes == (4, 2, 4) else general_shards
    return jax.shard_map(
        body,
        mesh=mesh,
        in_specs=placed,
        out_specs=(
            P("batch", "blk", None),
            P("batch", "blk", None),
            P(None, None, ("blk", "batch"), "tensor"),
            P(None, None, "tensor"),
            P(None, "tensor", ("blk", "batch")),
            P(None, ("blk", "batch"), "tensor"),
            P(None, "tensor"),
            P(None, "tensor", ("blk", "batch")),
            P(),
            P(),
            P(),
            P(),
        ),
        check_vma=False,
    )
```

profile of v0, /device:TPU:0, one launch (start us, length us, event | category | flops | bytes accessed | tf_op | source)
XLA Modules:
  0.0 96.9 jit_solution(754636921364793512)
XLA Ops:
  0.6 92.8 %encoder_layer.1 = (bf16[3,128,768]{2,1,0:T(8,128)(2,1)}, bf16[3,128,768]{2,1,0:T(8,128)(2,1)}, f32[96,576]{1,0:T(8,128)}, f32[96,192]{1,0:T(8,128)}, f32[96,768...) custom-call(s32[3]{0:T(128)} %bucket.1, s32[3,4]{1,0:T(4,128)} %refs_1_.1, ...), custom_call_target="tpu_custom_call" | custom-call | tf_op jit(solution)/shard_map/encoder_layer/pallas_call | solution.py:1211
  93.5 3.2 %finish.1 = (bf16[3,128,768]{2,1,0:T(8,128)(2,1)}, f32[3,128,768]{2,1,0:T(8,128)}, f32[3,96,192]{2,1,0:T(8,128)}, f32[2,192]{1,0:T(2,128)}, f32[192,96]{1,0:T(8,...) custom-call(s32[3]{0:T(128)} %bucket.1, ...), custom_call_target="tpu_custom_call" | custom-call | tf_op jit(solution)/shard_map/finish/pallas_call | solution.py:1236
where the time goes:
time: 97.1 us; the launch traced here: 96.9 us
  Pallas kernels  96.1 us (99%)
    pallas_call x1, Pallas kernels, fused_shards(): pl.pallas_call(fused_kernel, out_shape=main_out, in_specs=[smem, smem] +...  92.8 us
    pallas_call x1, Pallas kernels, fused_shards(): pl.pallas_call(finish_kernel, out_shape=[shape(n_seq, n_rows, width, dtyp...  3.24 us

commit v1 on v0

--- a/solution.py
+++ b/solution.py
@@ -675,6 +675,10 @@
         d = d.astype(BF16)
         dfb[here] = d
         tally(0, d.astype(F32))
+
+    def feed_back(s):
+        here = few_at(s)
+        d = dfb[here]
         total = jnp.zeros((half, width), F32)
         for k in range(2):
             p = (dot_nn(d, w_f[k]) * gp[k, here]).astype(BF16)
@@ -716,9 +720,10 @@
             grads(left[...], right[:, cols], rs.g.at[:, :, :, :, cols])
         rs.core()
 
+    def turn_d():
+        df_t[...] = jnp.transpose(dfb[...])
+
     def grad_f(k):
-        if k == 1:
-            df_t[...] = jnp.transpose(dfb[...])
         grads_wide(df_t, act.at[k], rs_f[k])
 
     def grad_i(k):
@@ -905,129 +910,133 @@
 
     weights_first()
     enter()
+    ga_o[0].issue()
     far_weight("o", w_o.at[0, own], w_o)
+    far_weight("f", ffo_w, w_f)
     ga_q.issue()
     ga_i[0].issue(ffi_w)
-    far_weight("i", ffi_w, w_i)
+    ga_o[0].forward_y()
+    ga_o[0].forward_x()
     ga_q.forward_y()
     ga_q.forward_x()
-    ga_o[0].issue()
     issue_second("o", ga_o[1])
+    far_weight("i", ffi_w, w_i)
+    ga_i[0].forward_x()
+    ga_i[0].forward_y()
+    ga_o[0].last()
     ga_f[0].issue(ffo_w)
-    ga_i[0].forward_y()
-    far_weight("f", ffo_w, w_f)
+    ga_o[1].forward_x()
     ga_q.last()
+    ga_o[1].forward_y()
     keys_values()
     queries()
-    ga_o[0].forward_x()
-    ga_o[1].forward_y()
+    issue_second("i", ga_i[1])
     attend(1)
-    ga_o[1].forward_x()
-    issue_second("i", ga_i[1])
-    ga_o[0].forward_y()
+    issue_second("f", ga_f[1])
     attend(2)
-    ga_i[0].forward_x()
+    ga_o[1].last()
     keys_pass()
     attend(0)
-    issue_second("f", ga_f[1])
+    project(1)
+    project(2)
     ga_i[1].forward_x()
-    ga_o[0].last()
     ga_f[0].forward_x()
-    ga_o[1].last()
-    project(2)
+    ga_i[0].last()
     ga_i[1].forward_y()
-    project(1)
-    ga_i[0].last()
     ga_f[0].forward_y()
     ga_f[1].forward_x()
+    ga_f[1].forward_y()
     project(0)
-    ga_f[1].forward_y()
-    turn_x()
     ga_i[1].last()
+    first_norm(1)
+    hidden(1)
+    feed_out(0, 1)
     first_norm(2)
     hidden(2)
     ga_f[0].last()
     feed_out(0, 2)
-    first_norm(1)
-    hidden(1)
     ga_f[1].last()
-    feed_out(0, 1)
     feed_out(1, 1)
+    feed_out(1, 2)
     first_norm(0)
-    feed_out(1, 2)
     hidden(0)
+    turn_y()
     feed_out(0, 0)
     feed_out(1, 0)
     second_norm(1)
+    feed_back(1)
     second_norm(2)
+    out_far(2)
+    feed_back(2)
+    turn_x()
     second_norm(0)
+    turn_d()
+    grad_f(1)
+    feed_back(0)
+    grad_i(1)
+    rs_f[1].first()
+    out_far(0)
+    grad_i(0)
+    first_norm_back(1)
+    rs_i[1].first()
+    grad_f(0)
+    first_norm_back(2)
+    first_norm_back(0)
+    grad_o()
+    rs_f[1].second_y()
+    out_near(0)
     out_far(1)
-    grad_f(1)
-    turn_y()
-    grad_i(0)
-    rs_f[1].first()
-    first_norm_back(1)
-    first_norm_back(2)
-    grad_i(1)
-    first_norm_back(0)
     vec_step(0)
-    vec_step(1)
-    out_far(0)
-    rs_f[1].second_y()
     rs_f[1].second_x()
-    out_near(1)
     attend_back(1)
-    rs_i[0].first()
-    out_far(2)
     attend_back(2)
     dx_first("b")
+    vec_step(1)
     attend_back(0)
-    grad_o()
     to_z("f", rs_f[1], t_f, z_f)
     keys_back()
+    vec_step(2)
     rs_o[1].first()
-    rs_i[0].second_y()
-    rs_i[1].first()
+    rs_f[0].first()
+    rs_i[1].second_x()
     dx_first("a")
+    dx_second("b")
+    grad_q()
     rs_o[0].first()
-    grad_f(0)
+    rs_o[1].second_x()
+    vec_step(3)
+    rs_q.first()
+    out_near(2)
+    rs_i[1].second_y()
+    dx_second("a")
+    dx_third("b")
+    out_near(1)
+    rs_i[0].first()
+    rs_q.second_x()
+    dx_third("a")
+    rs_o[0].second_y()
+    rs_o[0].second_x()
+    rs_q.second_y()
+    bias_step(0)
+    bias_step(1)
+    vec_store()
     rs_o[1].second_y()
-    dx_second("b")
-    out_near(0)
-    rs_o[1].second_x()
-    bias_step(0)
-    rs_f[0].first()
-    dx_second("a")
-    bias_step(1)
-    vec_step(2)
-    rs_i[0].second_x()
-    rs_i[1].second_y()
-    rs_i[1].second_x()
-    dx_third("b")
-    dx_third("a")
-    grad_q()
-    rs_q.first()
-    to_z("o", rs_o[1], t_o, z_o)
-    bias_step(2)
-    out_near(2)
-    rs_f[0].second_y()
+    rs_f[0].second_x()
     to_z("i", rs_i[1], t_i, z_i)
     dx_last("b")
-    rs_o[0].second_x()
-    rs_f[0].second_x()
-    rs_o[0].second_y()
     dx_last("a")
-    vec_step(3)
-    rs_q.second_y()
+    bias_step(2)
+    rs_f[0].second_y()
+    to_z("o", rs_o[1], t_o, z_o)
+    rs_i[0].second_y()
+    rs_i[0].second_x()
+    put("q", rs_q, gq_v, gq_hbm)
+    bias_store()
     out_store()
-    bias_store()
-    rs_q.second_x()
     put("f", rs_f[0], gf_v, gf_hbm, z_f)
-    put("q", rs_q, gq_v, gq_hbm)
-    put("o", rs_o[0], go_v, go_hbm, z_o)
     dx_store()
     put("i", rs_i[0], gi_v, gi_hbm, z_i)
-    vec_store()
+    put("o", rs_o[0], go_v, go_hbm, z_o)
 
     for copy in stores:
         copy.wait()

time: 97.1 us -> 95.7 us (0.986)
  Pallas kernels: 96.1 us -> 94.7 us
    pallas_call x1, Pallas kernels: 92.8 us -> 91.4 us  [fused_shards(): pl.pallas_call(fused_kernel, out_shape=main_out, in_specs=[smem, smem] +...]
where the time goes in v1:
time: 95.7 us; the launch traced here: 95.5 us
  Pallas kernels  94.7 us (99%)
    pallas_call x1, Pallas kernels, fused_shards(): pl.pallas_call(fused_kernel, out_shape=main_out, in_specs=[smem, smem] +...  91.4 us
    pallas_call x1, Pallas kernels, fused_shards(): pl.pallas_call(finish_kernel, out_shape=[shape(n_seq, n_rows, width, dtyp...  3.24 us

profile of v1, /device:TPU:0, one launch (start us, length us, event | category | flops | bytes accessed | tf_op | source)
XLA Modules:
  0.0 95.5 jit_solution(14735606906203928881)
XLA Ops:
  0.6 91.4 %encoder_layer.1 = (bf16[3,128,768]{2,1,0:T(8,128)(2,1)}, bf16[3,128,768]{2,1,0:T(8,128)(2,1)}, f32[96,576]{1,0:T(8,128)}, f32[96,192]{1,0:T(8,128)}, f32[96,768...) custom-call(s32[3]{0:T(128)} %bucket.1, s32[3,4]{1,0:T(4,128)} %refs_1_.1, ...), custom_call_target="tpu_custom_call" | custom-call | tf_op jit(solution)/shard_map/encoder_layer/pallas_call | solution.py:1220
  92.1 3.2 %finish.1 = (bf16[3,128,768]{2,1,0:T(8,128)(2,1)}, f32[3,128,768]{2,1,0:T(8,128)}, f32[3,96,192]{2,1,0:T(8,128)}, f32[2,192]{1,0:T(2,128)}, f32[192,96]{1,0:T(8,...) custom-call(s32[3]{0:T(128)} %bucket.1, ...), custom_call_target="tpu_custom_call" | custom-call | tf_op jit(solution)/shard_map/finish/pallas_call | solution.py:1245

commit v2 on v1

--- a/solution.py
+++ b/solution.py
@@ -489,10 +489,14 @@
     order = slot_order(bucket)
 
     def weights_first():
+        local[2].wait()
+        w_q[own] = jnp.concatenate([own_q[1], own_q[2], own_q[0]], 1)
+
+    def out_weight_turn():
         local[0].wait()
         w_o[0, own] = jnp.transpose(own_o[...])
-        local[2].wait()
-        w_q[own] = jnp.concatenate([own_q[1], own_q[2], own_q[0]], 1)
+
+    def tokens_in_order():
         local[1].wait()
         for s in range(n_seq):
             xs[s * n_rows : (s + 1) * n_rows] = tok[order[s]]
@@ -904,16 +908,18 @@
 
     def dx_store():
         for group in groups:
+            lo, hi = groups[group]
             for k in (4, 5):
                 st[group, k].wait_recv()
-        store(tg_v, tg_hbm)
+            store(tg_v.at[lo:hi], tg_hbm.at[lo:hi])
 
     weights_first()
     enter()
+    ga_q.issue()
+    out_weight_turn()
     ga_o[0].issue()
     far_weight("o", w_o.at[0, own], w_o)
     far_weight("f", ffo_w, w_f)
-    ga_q.issue()
     ga_i[0].issue(ffi_w)
     ga_o[0].forward_y()
     ga_o[0].forward_x()
@@ -928,6 +934,7 @@
     ga_o[1].forward_x()
     ga_q.last()
     ga_o[1].forward_y()
+    tokens_in_order()
     keys_values()
     queries()
     issue_second("i", ga_i[1])
@@ -1199,7 +1206,7 @@
         f(*wide["f"]),
         f(8, width),
         f(8, head_w),
-        pltpu.SemaphoreType.DMA((14,)),
+        pltpu.SemaphoreType.DMA((15,)),
         pltpu.SemaphoreType.DMA((N_SEND,)),
         pltpu.SemaphoreType.DMA((N_RECV,)),
     ]

time: 95.7 us -> 95.5 us (level)
  no operation moved by 1% of the time
where the time goes in v2:
time: 95.5 us; the launch traced here: 95.3 us
  Pallas kernels  94.5 us (99%)
    pallas_call x1, Pallas kernels, fused_shards(): pl.pallas_call(fused_kernel, out_shape=main_out, in_specs=[smem, smem] +...  91.2 us
    pallas_call x1, Pallas kernels, fused_shards(): pl.pallas_call(finish_kernel, out_shape=[shape(n_seq, n_rows, width, dtyp...  3.24 us

profile of v2, /device:TPU:0, one launch (start us, length us, event | category | flops | bytes accessed | tf_op | source)
XLA Modules:
  0.0 95.3 jit_solution(11713638040148217462)
XLA Ops:
  0.6 91.2 %encoder_layer.1 = (bf16[3,128,768]{2,1,0:T(8,128)(2,1)}, bf16[3,128,768]{2,1,0:T(8,128)(2,1)}, f32[96,576]{1,0:T(8,128)}, f32[96,192]{1,0:T(8,128)}, f32[96,768...) custom-call(s32[3]{0:T(128)} %bucket.1, s32[3,4]{1,0:T(4,128)} %refs_1_.1, ...), custom_call_target="tpu_custom_call" | custom-call | tf_op jit(solution)/shard_map/encoder_layer/pallas_call | solution.py:1227
  91.9 3.2 %finish.1 = (bf16[3,128,768]{2,1,0:T(8,128)(2,1)}, f32[3,128,768]{2,1,0:T(8,128)}, f32[3,96,192]{2,1,0:T(8,128)}, f32[2,192]{1,0:T(2,128)}, f32[192,96]{1,0:T(8,...) custom-call(s32[3]{0:T(128)} %bucket.1, ...), custom_call_target="tpu_custom_call" | custom-call | tf_op jit(solution)/shard_map/finish/pallas_call | solution.py:1252
